TPU v7x, 128 devices: a whole 4x4x4 slice. The times are simulated.
128 devices in a mesh: expert: 16 (over z, y), fsdp: 8 (over x, core).
Axes of the slice: x: 4, y: 4, z: 4, core: 2. Of those that a mesh axis runs over, the one named last changes fastest.
Arguments:
- tokens: bfloat16 [2, 8, 2048, 1024], P(None, 'fsdp', 'expert'), may hold values from -6 to 6
- cotangent: bfloat16 [2, 8, 2048, 1024], P(None, 'fsdp', 'expert'), may hold values from -6 to 6
- doc_lengths: int32 [2, 8, 3], P(None, 'fsdp'), may hold values from 1 to 2046, as said below
- routes: int32 [2, 8, 2048, 2], P(None, 'fsdp', 'expert'), may hold values from 0 to 15, all different within a row
- order: int32 [2, 8, 16, 256], P(None, 'fsdp', 'expert'), may hold values from 0 to 255, each once within a row
- gain_attn: bfloat16 [1024], P(('expert', 'fsdp')), may hold values from 0.5 to 1.5
- w_query: bfloat16 [1024, 1024], P(('expert', 'fsdp')), may hold values from -0.1875 to 0.1875
- w_key: bfloat16 [1024, 1024], P(('expert', 'fsdp')), may hold values from -0.1875 to 0.1875
- w_value: bfloat16 [1024, 1024], P(('expert', 'fsdp')), may hold values from -0.1875 to 0.1875
- w_out: bfloat16 [1024, 1024], P(('expert', 'fsdp')), may hold values from -1 to 1
- rel_table: bfloat16 [512], P(('expert', 'fsdp')), may hold values from -3 to 3
- gain_moe: bfloat16 [1024], P(('expert', 'fsdp')), may hold values from 0.5 to 1.5
- w_router: bfloat16 [1024, 16], P(('expert', 'fsdp')), may hold values from -0.125 to 0.125
- w_gate: bfloat16 [16, 1024, 2816], P('expert', None, 'fsdp'), may hold values from -0.1875 to 0.1875
- w_up: bfloat16 [16, 1024, 2816], P('expert', None, 'fsdp'), may hold values from -0.1875 to 0.1875
- w_down: bfloat16 [16, 2816, 1024], P('expert', 'fsdp'), may hold values from -0.15625 to 0.15625
Outputs:
- output: bfloat16 [2, 8, 2048, 1024], P(None, 'fsdp', 'expert')
- input_grad: bfloat16 [2, 8, 2048, 1024], P(None, 'fsdp', 'expert')
- grad_gain_attn: float32 [1024], P(('expert', 'fsdp'))
- grad_query: float32 [1024, 1024], P(('expert', 'fsdp'))
- grad_key: float32 [1024, 1024], P(('expert', 'fsdp'))
- grad_value: float32 [1024, 1024], P(('expert', 'fsdp'))
- grad_out: float32 [1024, 1024], P(('expert', 'fsdp'))
- grad_table: float32 [512], P(('expert', 'fsdp'))
- grad_gain_moe: float32 [1024], P(('expert', 'fsdp'))
- grad_router: float32 [1024, 16], P(('expert', 'fsdp'))
- grad_gate: float32 [16, 1024, 2816], P('expert', None, 'fsdp')
- grad_up: float32 [16, 1024, 2816], P('expert', None, 'fsdp')
- grad_down: float32 [16, 2816, 1024], P('expert', 'fsdp')
Inputs may be any that keep to these rules, and one draw needn't show every extreme that they name: `doc_lengths`: in each sequence the first and last documents are shorter than 128 tokens and the middle one holds the rest; in some sequence the first and last documents hold one token each. The two routes of a token differ. Each block's slots in an order of precedence, each number once.
All inputs are finite; a program needn't handle non-finite values.
Results may differ from a plain program's by a relative error of at most 0.035.
Values may be sent and summed in bfloat16 or wider, within the bound.
A program may use at most 256 MiB of HBM per device.

v0:
```python
import jax
import jax.numpy as jnp
from jax import lax
from jax.sharding import PartitionSpec as P

H = 16
NB = 32
WINDOW = 1024


EPS = 1e-06
MASKED = -1e30
THRESHOLDS = (19, 21, 24, 27, 31, 35, 40, 46, 52, 59, 67, 77, 87, 99, 113)
highest = lax.Precision.HIGHEST


def rms_norm(values, gain_vec):
    factor = lax.rsqrt(jnp.mean(values * values, axis=-1, keepdims=True) + EPS)
    return values * factor * gain_vec


def buckets(distance):
    beyond = 16 + sum(((distance >= boundary).astype(jnp.int32) for boundary in THRESHOLDS))
    return jnp.where(distance < 16, distance, beyond)


def document_index(lengths, position):
    first_end = lengths[..., 0:1]
    second_end = first_end + lengths[..., 1:2]
    return (position >= first_end).astype(jnp.int32) + (position >= second_end).astype(jnp.int32)


def dot_plain(left, right):
    return jnp.dot(left, right, preferred_element_type=jnp.float32)


def product_right_transposed(left, right):
    return lax.dot_general(
        left, right, (((1,), (1,)), ((), ())), preferred_element_type=jnp.float32
    )


def dot_left_t(left, right):
    return lax.dot_general(
        left, right, (((0,), (0,)), ((), ())), preferred_element_type=jnp.float32
    )


def gated_unit(gate_pre, up_pre):
    return jax.nn.gelu(gate_pre, approximate=True) * up_pre


def add_all(first_group, second_group):
    if first_group is None:
        return second_group
    return tuple((left_val + right_val for left_val, right_val in zip(first_group, second_group)))


def exchanged(payload):
    return lax.all_to_all(payload, "expert", split_axis=0, concat_axis=0, tiled=True)


def fetch_shared(gain_attn, w_query, w_key, w_value, w_out, rel_table, gain_moe, w_router):
    return (
        lax.all_gather(gain_attn, ("expert", "fsdp"), axis=0, tiled=True),
        lax.all_gather(w_query, ("expert", "fsdp"), axis=0, tiled=True),
        lax.all_gather(w_key, ("expert", "fsdp"), axis=0, tiled=True),
        lax.all_gather(w_value, ("expert", "fsdp"), axis=0, tiled=True),
        lax.all_gather(w_out, ("expert", "fsdp"), axis=0, tiled=True),
        lax.all_gather(rel_table, ("expert", "fsdp"), axis=0, tiled=True),
        lax.all_gather(gain_moe, ("expert", "fsdp"), axis=0, tiled=True),
        lax.all_gather(w_router, ("expert", "fsdp"), axis=0, tiled=True),
    )


def reduce_shared(terms):
    return (
        lax.psum_scatter(terms[0], ("expert", "fsdp"), scatter_dimension=0, tiled=True),
        lax.psum_scatter(terms[1], ("expert", "fsdp"), scatter_dimension=0, tiled=True),
        lax.psum_scatter(terms[2], ("expert", "fsdp"), scatter_dimension=0, tiled=True),
        lax.psum_scatter(terms[3], ("expert", "fsdp"), scatter_dimension=0, tiled=True),
        lax.psum_scatter(terms[4], ("expert", "fsdp"), scatter_dimension=0, tiled=True),
        lax.psum_scatter(terms[5], ("expert", "fsdp"), scatter_dimension=0, tiled=True),
        lax.psum_scatter(terms[6], ("expert", "fsdp"), scatter_dimension=0, tiled=True),
        lax.psum_scatter(terms[7], ("expert", "fsdp"), scatter_dimension=0, tiled=True),
    )


def reduce_expert(terms):
    return (
        lax.psum_scatter(
            terms[0].astype(jnp.bfloat16), "fsdp", scatter_dimension=2, tiled=True
        ).astype(jnp.float32),
        lax.psum_scatter(
            terms[1].astype(jnp.bfloat16), "fsdp", scatter_dimension=2, tiled=True
        ).astype(jnp.float32),
        lax.psum_scatter(
            terms[2].astype(jnp.bfloat16), "fsdp", scatter_dimension=1, tiled=True
        ).astype(jnp.float32),
    )


def attention_scores(queries, key_rows, lengths, position_bias_lookup, query_offset, key_offset):
    groups, query_len, model_width = queries.shape
    key_len = key_rows.shape[1]
    head_dim = model_width // H
    query_heads = queries.reshape(groups, query_len, H, head_dim)
    key_heads = key_rows.reshape(groups, key_len, H, head_dim)
    raw_scores = jnp.einsum(
        "gqhd,gkhd->ghqk", query_heads, key_heads, preferred_element_type=jnp.float32
    ) * head_dim ** (-0.5)
    query_pos = query_offset + jnp.arange(query_len, dtype=jnp.int32)
    key_pos = key_offset + jnp.arange(key_len, dtype=jnp.int32)
    distance = query_pos[:, None] - key_pos[None, :]
    bucket_ids = buckets(jnp.maximum(distance, 0))
    single_hot_matrix = (bucket_ids[None] == jnp.arange(NB, dtype=jnp.int32)[:, None, None]).astype(
        jnp.bfloat16
    )
    relative_offset_bias = jnp.einsum(
        "yao,iy->iao", single_hot_matrix, position_bias_lookup, preferred_element_type=jnp.float32
    )
    query_doc = document_index(lengths, query_pos)
    key_doc = document_index(lengths, key_pos)
    allowed = (
        (query_doc[:, :, None] == key_doc[:, None, :])
        & (distance >= 0)[None]
        & (distance < WINDOW)[None]
    )
    scores = jnp.where(allowed[:, None], raw_scores + relative_offset_bias[None], MASKED)
    return (scores, single_hot_matrix)


def on_device(
    tokens,
    cotangent,
    doc_lengths,
    routes,
    order,
    gain_attn,
    w_query,
    w_key,
    w_value,
    w_out,
    rel_table,
    gain_moe,
    w_router,
    w_gate,
    w_up,
    w_down,
):
    micro_count, groups, length, model_width = tokens.shape
    expert_count = lax.axis_size("expert")
    row_count = groups * length
    slot_count = 2 * row_count
    seq_len = length * expert_count
    head_dim = model_width // H
    score_scale = head_dim ** (-0.5)
    window_span = WINDOW + length
    capacity = max(2, (5 * row_count + 2 * expert_count - 1) // (2 * expert_count))
    buffer_rows = expert_count * capacity
    offset = lax.axis_index("expert") * length
    key_start = jnp.maximum(offset - WINDOW, 0)
    full_gate, full_up, full_down = (
        lax.all_gather(w_gate, "fsdp", axis=2, tiled=True),
        lax.all_gather(w_up, "fsdp", axis=2, tiled=True),
        lax.all_gather(w_down, "fsdp", axis=1, tiled=True),
    )
    gate_w, up_w, down_w = (full_gate[0], full_up[0], full_down[0])
    outputs_list = []
    grads_list = []
    shared_acc = None
    expert_acc = None
    for micro_step in range(micro_count):
        (
            attn_gain,
            query_full,
            key_full,
            complete_value_rows,
            output_full,
            table_full,
            moe_gain,
            router_full,
        ) = fetch_shared(gain_attn, w_query, w_key, w_value, w_out, rel_table, gain_moe, w_router)
        position_bias_lookup = table_full.reshape(H, NB)
        lengths = doc_lengths[micro_step]
        hidden_in = tokens[micro_step].reshape(row_count, model_width).astype(jnp.float32)
        normed_f, norm_back_one = jax.vjp(rms_norm, hidden_in, attn_gain.astype(jnp.float32))
        normed = normed_f.astype(jnp.bfloat16)
        queries = dot_plain(normed, query_full).astype(jnp.bfloat16)
        keys_own = dot_plain(normed, key_full).astype(jnp.bfloat16)
        values_own = dot_plain(normed, complete_value_rows).astype(jnp.bfloat16)
        keys_all, values_all = (
            lax.all_gather(
                keys_own.reshape(groups, length, model_width), "expert", axis=1, tiled=True
            ),
            lax.all_gather(
                values_own.reshape(groups, length, model_width), "expert", axis=1, tiled=True
            ),
        )
        keys_near = lax.dynamic_slice_in_dim(keys_all, key_start, window_span, 1)
        values_near = lax.dynamic_slice_in_dim(values_all, key_start, window_span, 1)
        query_group = queries.reshape(groups, length, model_width)
        scores, single_hot_matrix = attention_scores(
            query_group, keys_near, lengths, position_bias_lookup, offset, key_start
        )
        top_score = jnp.max(scores, axis=-1, keepdims=True)
        exponent = jnp.exp(scores - top_score)
        denominator = jnp.sum(exponent, axis=-1, keepdims=True)
        attn_probs = exponent / denominator
        log_total = top_score + jnp.log(denominator)
        value_heads = values_near.reshape(groups, window_span, H, head_dim)
        attended = (
            jnp.einsum(
                "ghqk,gkhd->gqhd",
                attn_probs.astype(jnp.bfloat16),
                value_heads,
                preferred_element_type=jnp.float32,
            )
            .reshape(row_count, model_width)
            .astype(jnp.bfloat16)
        )
        hidden = hidden_in + dot_plain(attended, output_full)
        mixed_f, norm_back_two = jax.vjp(rms_norm, hidden, moe_gain.astype(jnp.float32))
        mixed_rows = mixed_f.astype(jnp.bfloat16)
        logits = dot_plain(mixed_rows, router_full)
        route_now = routes[micro_step].reshape(row_count, 2)
        route_match = (route_now[:, :, None] == jnp.arange(expert_count, dtype=jnp.int32)).astype(
            jnp.float32
        )

        def gate_pair(logit_in):
            chance = jax.nn.softmax(logit_in, axis=-1)
            chosen = jnp.sum(route_match * chance[:, None, :], axis=-1)
            return chosen / jnp.sum(chosen, axis=-1, keepdims=True)

        gate_share, share_back = jax.vjp(gate_pair, logits)
        slot_expert = route_now.reshape(slot_count)
        precedence = order[micro_step].reshape(slot_count)
        same_expert = slot_expert[:, None] == slot_expert[None, :]
        earlier = precedence[None, :] < precedence[:, None]
        slot_rank = jnp.sum((same_expert & earlier).astype(jnp.int32), axis=1)
        target = jnp.where(slot_rank < capacity, slot_expert * capacity + slot_rank, buffer_rows)
        placing = jnp.arange(buffer_rows, dtype=jnp.int32)[:, None] == target[None, :]
        place_slots = placing.astype(jnp.bfloat16)
        place_tokens = jnp.any(placing.reshape(buffer_rows, row_count, 2), axis=-1).astype(
            jnp.bfloat16
        )
        send_rows = (
            dot_plain(place_tokens, mixed_rows)
            .astype(jnp.bfloat16)
            .reshape(expert_count, capacity, model_width)
        )
        received = exchanged(send_rows).reshape(buffer_rows, model_width)
        gate_pre = dot_plain(received, gate_w)
        up_pre = dot_plain(received, up_w)
        activated, unit_back = jax.vjp(gated_unit, gate_pre, up_pre)
        activated_b = activated.astype(jnp.bfloat16)
        expert_out = dot_plain(activated_b, down_w).astype(jnp.bfloat16)
        returned = exchanged(expert_out.reshape(expert_count, capacity, model_width)).reshape(
            buffer_rows, model_width
        )
        slot_out = dot_left_t(place_slots, returned).reshape(row_count, 2, model_width)
        result = hidden + jnp.sum(slot_out * gate_share[:, :, None], axis=1)
        outputs_list.append(result.astype(jnp.bfloat16).reshape(groups, length, model_width))
        grad_out = cotangent[micro_step].reshape(row_count, model_width).astype(jnp.float32)
        slot_grad = (
            (gate_share[:, :, None] * grad_out[:, None, :])
            .reshape(slot_count, model_width)
            .astype(jnp.bfloat16)
        )
        share_grad = jnp.sum(slot_out * grad_out[:, None, :], axis=-1)
        (logit_grad,) = share_back(share_grad)
        send_grad = (
            dot_plain(place_slots, slot_grad)
            .astype(jnp.bfloat16)
            .reshape(expert_count, capacity, model_width)
        )
        received_grad = exchanged(send_grad).reshape(buffer_rows, model_width)
        act_grad = product_right_transposed(received_grad, down_w).astype(jnp.bfloat16)
        down_w_grad = dot_left_t(activated_b, received_grad)
        gate_grad_f, up_grad_f = unit_back(act_grad.astype(jnp.float32))
        gate_grad = gate_grad_f.astype(jnp.bfloat16)
        up_grad = up_grad_f.astype(jnp.bfloat16)
        gate_w_grad = dot_left_t(received, gate_grad)
        up_w_grad = dot_left_t(received, up_grad)
        row_grad = (
            product_right_transposed(gate_grad, gate_w) + product_right_transposed(up_grad, up_w)
        ).astype(jnp.bfloat16)
        returned_grad = exchanged(row_grad.reshape(expert_count, capacity, model_width)).reshape(
            buffer_rows, model_width
        )
        router_f = router_full.astype(jnp.float32)
        mixed_grad = dot_left_t(place_tokens, returned_grad) + lax.dot_general(
            logit_grad, router_f, (((1,), (1,)), ((), ())), precision=highest
        )
        router_grad = lax.dot_general(
            mixed_rows.astype(jnp.float32), logit_grad, (((0,), (0,)), ((), ())), precision=highest
        )
        hidden_norm_grad, moe_gain_grad = norm_back_two(mixed_grad)
        hidden_grad = grad_out + hidden_norm_grad
        branch_grad = hidden_grad.astype(jnp.bfloat16)
        out_w_grad = dot_left_t(attended, branch_grad)
        attended_grad = product_right_transposed(branch_grad, output_full).astype(jnp.bfloat16)
        scores, single_hot_matrix = attention_scores(
            query_group, keys_near, lengths, position_bias_lookup, offset, key_start
        )
        attn_probs = jnp.exp(scores - log_total)
        grad_heads = attended_grad.reshape(groups, length, H, head_dim)
        prob_grad = jnp.einsum(
            "gqhd,gkhd->ghqk", grad_heads, value_heads, preferred_element_type=jnp.float32
        )
        row_inner = jnp.sum(attn_probs * prob_grad, axis=-1, keepdims=True)
        attention_score_gradient = (attn_probs * (prob_grad - row_inner)).astype(jnp.bfloat16)
        key_heads = keys_near.reshape(groups, window_span, H, head_dim)
        query_heads = query_group.reshape(groups, length, H, head_dim)
        query_grad = (
            (
                jnp.einsum(
                    "ghqk,gkhd->gqhd",
                    attention_score_gradient,
                    key_heads,
                    preferred_element_type=jnp.float32,
                )
                * score_scale
            )
            .reshape(row_count, model_width)
            .astype(jnp.bfloat16)
        )
        table_grad = jnp.einsum(
            "pty,xdty->dp",
            single_hot_matrix,
            attention_score_gradient,
            preferred_element_type=jnp.float32,
        )
        value_part = jnp.einsum(
            "ghqk,gqhd->gkhd",
            attn_probs.astype(jnp.bfloat16),
            grad_heads,
            preferred_element_type=jnp.float32,
        ).reshape(groups, window_span, model_width)
        key_part = (
            jnp.einsum(
                "ghqk,gqhd->gkhd",
                attention_score_gradient,
                query_heads,
                preferred_element_type=jnp.float32,
            )
            * score_scale
        ).reshape(groups, window_span, model_width)
        zero_rows = jnp.zeros((groups, seq_len, model_width), jnp.float32)
        key_placed = lax.dynamic_update_slice_in_dim(zero_rows, key_part, key_start, 1)
        value_placed = lax.dynamic_update_slice_in_dim(zero_rows, value_part, key_start, 1)
        key_sum, value_sum = (
            lax.psum_scatter(
                key_placed.astype(jnp.bfloat16), "expert", scatter_dimension=1, tiled=True
            ).astype(jnp.float32),
            lax.psum_scatter(
                value_placed.astype(jnp.bfloat16), "expert", scatter_dimension=1, tiled=True
            ).astype(jnp.float32),
        )
        key_grad = key_sum.reshape(row_count, model_width).astype(jnp.bfloat16)
        value_grad = value_sum.reshape(row_count, model_width).astype(jnp.bfloat16)
        query_w_grad = dot_left_t(normed, query_grad)
        key_w_grad = dot_left_t(normed, key_grad)
        value_weight_gradient = dot_left_t(normed, value_grad)
        normed_grad = (
            product_right_transposed(query_grad, query_full)
            + product_right_transposed(key_grad, key_full)
            + product_right_transposed(value_grad, complete_value_rows)
        )
        input_norm_grad, attn_gain_grad = norm_back_one(normed_grad)
        input_grad = hidden_grad + input_norm_grad
        grads_list.append(input_grad.astype(jnp.bfloat16).reshape(groups, length, model_width))
        shared_terms = (
            attn_gain_grad,
            query_w_grad,
            key_w_grad,
            value_weight_gradient,
            out_w_grad,
            table_grad.reshape(-1),
            moe_gain_grad,
            router_grad,
        )
        expert_terms = (gate_w_grad[None], up_w_grad[None], down_w_grad[None])
        shared_acc = add_all(shared_acc, reduce_shared(shared_terms))
        expert_acc = add_all(expert_acc, reduce_expert(expert_terms))
    return (
        jnp.stack(outputs_list),
        jnp.stack(grads_list),
        shared_acc[0],
        shared_acc[1],
        shared_acc[2],
        shared_acc[3],
        shared_acc[4],
        shared_acc[5],
        shared_acc[6],
        shared_acc[7],
        expert_acc[0],
        expert_acc[1],
        expert_acc[2],
    )


def solution(mesh):
    placed = (
        P(None, "fsdp", "expert", None),
        P(None, "fsdp", "expert", None),
        P(None, "fsdp", None),
        P(None, "fsdp", "expert", None),
        P(None, "fsdp", "expert", None),
        P(("expert", "fsdp")),
        P(("expert", "fsdp"), None),
        P(("expert", "fsdp"), None),
        P(("expert", "fsdp"), None),
        P(("expert", "fsdp"), None),
        P(("expert", "fsdp")),
        P(("expert", "fsdp")),
        P(("expert", "fsdp"), None),
        P("expert", None, "fsdp"),
        P("expert", None, "fsdp"),
        P("expert", "fsdp", None),
    )
    return jax.shard_map(
        on_device,
        mesh=mesh,
        in_specs=placed,
        out_specs=(
            P(None, "fsdp", "expert", None),
            P(None, "fsdp", "expert", None),
            P(("expert", "fsdp")),
            P(("expert", "fsdp"), None),
            P(("expert", "fsdp"), None),
            P(("expert", "fsdp"), None),
            P(("expert", "fsdp"), None),
            P(("expert", "fsdp")),
            P(("expert", "fsdp")),
            P(("expert", "fsdp"), None),
            P("expert", None, "fsdp"),
            P("expert", None, "fsdp"),
            P("expert", "fsdp", None),
        ),
        check_vma=False,
    )
```

profile of v0, /device:TPU:1, one launch (start us, length us, event | category | flops | bytes accessed | tf_op | source)
XLA Modules:
  0.0 4141.1 jit_solution(17984377957035796260)
XLA Ops:
  12.0 69.6 %all-reduce.8 = (bf16[1024]{0:T(1024)(128)(2,1)S(1)}, bf16[512]{0:T(512)(128)(2,1)S(1)}, bf16[1024]{0:T(1024)(128)(2,1)S(1)}) all-reduce(bf16[1024]{0:T(1024)(128)(2,1)S(1)} %dynamic-update-slice, bf16[512]{0:T(512)(128)(2,1)S(1)} %dynamic-update-slice.1, ...), channel_id=1, replica_groups=mesh['expert'=16,'fsdp'=8] {'expert','fsdp'}, use_global_device_ids=true, to_apply=%add | all-reduce | flops 2560 | bytes 10240
  85.9 60.2 %all-gather.16.cloned.1.call-done = bf16[1024,1024]{1,0:T(8,128)(2,1)} async-done(((bf16[8,1024]{1,0:T(8,128)(2,1)}), bf16[1024,1024]{1,0:T(8,128)(2,1)}) %all-gather.16.cloned.1.call-update) | async-done | bytes 2097168 | tf_op jit(solution)/shard_map/all_gather | solution.py:68
  168.2 33.3 all_gather.65
  219.3 44.0 %all-gather.32.cloned.1.call-done = bf16[2048,1024]{1,0:T(8,128)(2,1)} async-done(((bf16[128,1024]{1,0:T(8,128)(2,1)}), bf16[2048,1024]{1,0:T(8,128)(2,1)}) %all-gather.32.cloned.1.call-update) | async-done | bytes 4194320 | tf_op jit(solution)/shard_map/all_gather | solution.py:193
  263.3 53.8 %all-gather.30.cloned.1.call-done = bf16[2048,1024]{1,0:T(8,128)(2,1)} async-done(((bf16[128,1024]{1,0:T(8,128)(2,1)}), bf16[2048,1024]{1,0:T(8,128)(2,1)}) %all-gather.30.cloned.1.call-update) | async-done | bytes 4194320 | tf_op jit(solution)/shard_map/all_gather | solution.py:196
  327.8 43.2 %all-gather.36.cloned.1.call-done = bf16[2048,1024]{1,0:T(8,128)(2,1)} async-done(((bf16[128,1024]{1,0:T(8,128)(2,1)}), bf16[2048,1024]{1,0:T(8,128)(2,1)}) %all-gather.36.cloned.1.call-update) | async-done | bytes 4194320 | tf_op jit(solution)/shard_map/all_gather | solution.py:193
  371.0 53.4 %all-gather.34.cloned.1.call-done = bf16[2048,1024]{1,0:T(8,128)(2,1)} async-done(((bf16[128,1024]{1,0:T(8,128)(2,1)}), bf16[2048,1024]{1,0:T(8,128)(2,1)}) %all-gather.34.cloned.1.call-update) | async-done | bytes 4194320 | tf_op jit(solution)/shard_map/all_gather | solution.py:196
  448.2 44.7 %all-gather.22.cloned.1.call-done = bf16[1024,1024]{1,0:T(8,128)(2,1)} async-done(((bf16[8,1024]{1,0:T(8,128)(2,1)}), bf16[1024,1024]{1,0:T(8,128)(2,1)}) %all-gather.22.cloned.1.call-update) | async-done | bytes 2097168 | tf_op jit(solution)/shard_map/all_gather | solution.py:69
  577.8 33.7 all-gather.24.cloned.1.call-done
  875.7 20.6 copy.127
  1023.5 26.5 copy.135
  1068.3 26.5 copy.139
  1110.7 26.5 copy.137
  1156.1 26.4 copy.141
  1262.6 49.6 %all-reduce.11.cloned.1.call-done = f32[1024,16]{1,0:T(8,128)} async-done(((f32[1024,16]{1,0:T(8,128)}), f32[1024,16]{1,0:T(8,128)}) %all-reduce.11.cloned.1.call-update) | async-done | bytes 65552
  1320.7 65.6 %all-reduce.7 = (f32[1024]{0:T(1024)S(1)}, f32[512]{0:T(512)S(1)}, f32[1024]{0:T(1024)S(1)}) all-reduce(f32[1024]{0:T(1024)S(1)} %add.562, f32[512]{0:T(512)S(1)} %reshape.1069, f32[1024]{0:T(1024)S(1)} %add.568), channel_id=18, replica_groups=mesh['expert'=16,'fsdp'=8] {'expert','fsdp'}, use_global_device_ids=true, to_apply=%region_41.42.clone | all-reduce | flops 2560 | bytes 20480
  1400.3 39.8 reduce-scatter.53.cloned.1.call-done
  1447.7 35.5 reduce-scatter.57.cloned.1.call-done
  1488.5 37.9 reduce-scatter.31.cloned.1.call-done
  1526.4 43.2 %reduce-scatter.33.cloned.1.call-done = bf16[1,352,1024]{2,1,0:T(8,128)(2,1)} async-done(((bf16[1,2816,1024]{2,1,0:T(8,128)(2,1)}), bf16[1,352,1024]{2,1,0:T(8,128)(2,1)}) %reduce-scatter.33.cloned.1.call-update) | async-done | bytes 720912 | tf_op jit(solution)/shard_map/reduce_scatter | solution.py:97
  1572.3 639.1 %reduce-scatter.35.cloned.1.call-done = f32[8,1024]{1,0:T(8,128)} async-done(((f32[1024,1024]{1,0:T(8,128)}), f32[8,1024]{1,0:T(8,128)}) %reduce-scatter.35.cloned.1.call-update) | async-done | bytes 32784 | tf_op jit(solution)/shard_map/reduce_scatter | solution.py:79
  2211.4 640.8 %reduce-scatter.41.cloned.1.call-done = f32[8,1024]{1,0:T(8,128)} async-done(((f32[1024,1024]{1,0:T(8,128)}), f32[8,1024]{1,0:T(8,128)}) %reduce-scatter.41.cloned.1.call-update) | async-done | bytes 32784 | tf_op jit(solution)/shard_map/reduce_scatter | solution.py:82
  2852.2 641.1 %reduce-scatter.37.cloned.1.call-done = f32[8,1024]{1,0:T(8,128)} async-done(((f32[1024,1024]{1,0:T(8,128)}), f32[8,1024]{1,0:T(8,128)}) %reduce-scatter.37.cloned.1.call-update) | async-done | bytes 32784 | tf_op jit(solution)/shard_map/reduce_scatter | solution.py:80
  3493.3 640.8 %reduce-scatter.39.cloned.1.call-done = f32[8,1024]{1,0:T(8,128)} async-done(((f32[1024,1024]{1,0:T(8,128)}), f32[8,1024]{1,0:T(8,128)}) %reduce-scatter.39.cloned.1.call-update) | async-done | bytes 32784 | tf_op jit(solution)/shard_map/reduce_scatter | solution.py:81
  (610 shorter events, 725.9 us)
Async XLA Ops:
  8.7 205.3 %all-gather.18.cloned.1.call-start = ((), (), s32[]{:S(2)}) async-start(), calls=%async_computation.23 | async-start | bytes 2113536 | tf_op jit(solution)/shard_map/all_gather | solution.py:66
  9.4 253.9 %all-gather.32.cloned.1.call-start = ((), (), s32[]{:S(2)}) async-start(), calls=%async_computation.32 | async-start | bytes 4456448 | tf_op jit(solution)/shard_map/all_gather | solution.py:193
  85.9 231.3 %all-gather.30.cloned.1.call-start = ((), (), s32[]{:S(2)}) async-start(), calls=%async_computation.31 | async-start | bytes 4456448 | tf_op jit(solution)/shard_map/all_gather | solution.py:196
  149.1 221.9 %all-gather.36.cloned.1.call-start = ((), (), s32[]{:S(2)}) async-start(), calls=%async_computation.34 | async-start | bytes 4456448 | tf_op jit(solution)/shard_map/all_gather | solution.py:193
  152.0 272.4 %all-gather.34.cloned.1.call-start = ((), (), s32[]{:S(2)}) async-start(), calls=%async_computation.33 | async-start | bytes 4456448 | tf_op jit(solution)/shard_map/all_gather | solution.py:196
  153.3 339.6 %all-gather.22.cloned.1.call-start = ((), (), s32[]{:S(2)}) async-start(), calls=%async_computation.25 | async-start | bytes 2113536 | tf_op jit(solution)/shard_map/all_gather | solution.py:69
  154.0 403.1 %all-gather.28.cloned.1.call-start = ((), (), s32[]{:S(2)}) async-start(), calls=%async_computation.28 | async-start | bytes 6488064 | tf_op jit(solution)/shard_map/all_gather | solution.py:166
  154.8 416.2 %all-gather.26.cloned.1.call-start = ((), (), s32[]{:S(2)}) async-start(), calls=%async_computation.27 | async-start | bytes 6488064 | tf_op jit(solution)/shard_map/all_gather | solution.py:165
  155.4 456.1 %all-gather.24.cloned.1.call-start = ((), (), s32[]{:S(2)}) async-start(), calls=%async_computation.26 | async-start | bytes 6488064 | tf_op jit(solution)/shard_map/all_gather | solution.py:164
  758.3 466.0 %reduce-scatter.47.cloned.1.call-start = ((), (), s32[]{:S(2)}) async-start(), calls=%async_computation.41 | async-start | bytes 4456448
  841.3 384.7 %reduce-scatter.43.cloned.1.call-start = ((), (), s32[]{:S(2)}) async-start(), calls=%async_computation.39 | async-start | bytes 4456448
  903.4 328.0 %reduce-scatter.49.cloned.1.call-start = ((), (), s32[]{:S(2)}) async-start(), calls=%async_computation.42 | async-start | bytes 4456448
  959.3 273.9 %reduce-scatter.45.cloned.1.call-start = ((), (), s32[]{:S(2)}) async-start(), calls=%async_computation.40 | async-start | bytes 4456448
  1014.3 297.9 %all-reduce.11.cloned.1.call-start = ((), (), s32[]{:S(2)}) async-start(), calls=%async_computation.47 | async-start | bytes 1048576
  1016.9 373.8 %reduce-scatter.51.cloned.1.call-start = ((), (), s32[]{:S(2)}) async-start(), calls=%async_computation.43 | async-start | bytes 6488064
  1059.2 337.5 %reduce-scatter.55.cloned.1.call-start = ((), (), s32[]{:S(2)}) async-start(), calls=%async_computation.45 | async-start | bytes 6488064
  1103.9 336.1 %reduce-scatter.53.cloned.1.call-start = ((), (), s32[]{:S(2)}) async-start(), calls=%async_computation.44 | async-start | bytes 6488064
  1146.4 336.8 %reduce-scatter.57.cloned.1.call-start = ((), (), s32[]{:S(2)}) async-start(), calls=%async_computation.46 | async-start | bytes 6488064
  1191.8 334.6 %reduce-scatter.31.cloned.1.call-start = ((), (), s32[]{:S(2)}) async-start(), calls=%async_computation.29 | async-start | bytes 6488064 | tf_op jit(solution)/shard_map/reduce_scatter | solution.py:97
  1198.5 371.1 %reduce-scatter.33.cloned.1.call-start = ((), (), s32[]{:S(2)}) async-start(), calls=%async_computation.30 | async-start | bytes 6488064 | tf_op jit(solution)/shard_map/reduce_scatter | solution.py:97
  1205.3 1006.2 %reduce-scatter.35.cloned.1.call-start = ((), (), s32[]{:S(2)}) async-start(), calls=%async_computation.35 | async-start | bytes 4227072 | tf_op jit(solution)/shard_map/reduce_scatter | solution.py:79
  1219.9 1632.3 %reduce-scatter.41.cloned.1.call-start = ((), (), s32[]{:S(2)}) async-start(), calls=%async_computation.38 | async-start | bytes 4227072 | tf_op jit(solution)/shard_map/reduce_scatter | solution.py:82
  1224.2 2269.1 %reduce-scatter.37.cloned.1.call-start = ((), (), s32[]{:S(2)}) async-start(), calls=%async_computation.36 | async-start | bytes 4227072 | tf_op jit(solution)/shard_map/reduce_scatter | solution.py:80
  1231.4 2902.7 %reduce-scatter.39.cloned.1.call-start = ((), (), s32[]{:S(2)}) async-start(), calls=%async_computation.37 | async-start | bytes 4227072 | tf_op jit(solution)/shard_map/reduce_scatter | solution.py:81
  (154 other events, 2947.7 us)
Sparse Core Ops, SparseCore 0:
  11.2 68.9 all-gather.19
  83.3 62.7 all-gather.15
  149.2 62.7 all-gather.17
  214.6 48.6 all-gather.31
  265.9 51.2 all-gather.29
  319.7 51.2 all-gather.35
  373.1 51.2 all-gather.33
  427.5 65.2 all-gather.21
  532.3 38.7 all-gather.25
  572.7 38.7 all-gather.23
  841.4 78.4 reduce-scatter.46
  923.5 77.0 reduce-scatter.42
  1003.8 77.0 reduce-scatter.48
  1084.4 77.0 reduce-scatter.44
  1166.1 146.1 all-reduce.10
  1355.7 40.9 reduce-scatter.54
  1399.2 40.7 reduce-scatter.52
  1442.4 40.6 reduce-scatter.56
  1485.7 40.6 reduce-scatter.30
  1528.9 40.6 reduce-scatter.32
  1572.7 638.7 reduce-scatter.34
  2214.2 637.9 reduce-scatter.40
  2855.3 637.9 reduce-scatter.36
  3496.1 637.9 reduce-scatter.38
  (2 shorter events, 74.6 us)
where the time goes:
time: 4170 us; the launch traced here: 4140 us
  waiting for transfers between devices  3150 us (76%)
  local copies, waits for them, and re-layouts  469 us (11%)
  matrix products  261 us (6%)
  blocking collectives  169 us (4%)
  starting transfers between devices  41.7 us (1%)
    reduce_scatter x1, waiting for transfers between devices, reduce_shared(): lax.psum_scatter(terms[2], ('expert', 'fsdp'), scatter_dimension=0, tiled...  641 us
    reduce_scatter x1, waiting for transfers between devices, reduce_shared(): lax.psum_scatter(terms[4], ('expert', 'fsdp'), scatter_dimension=0, tiled...  641 us
    reduce_scatter x1, waiting for transfers between devices, reduce_shared(): lax.psum_scatter(terms[3], ('expert', 'fsdp'), scatter_dimension=0, tiled...  641 us
    reduce_scatter x1, waiting for transfers between devices, reduce_shared(): lax.psum_scatter(terms[1], ('expert', 'fsdp'), scatter_dimension=0, tiled...  639 us
    unnamed x340, local copies, waits for them, and re-layouts  336 us
    unnamed x2, blocking collectives  135 us
    unnamed x35, waiting for transfers between devices  132 us
    all_gather x2, waiting for transfers between devices, on_device(): lax.all_gather(values_own.reshape(groups, length, model_width), 'expert',...  107 us
  transfers between devices with their start and end apart: 34, of which 25 were waited for; matrix products, arithmetic and copies ran while one was open for 15% of the time, Pallas kernels for 0%

commit v1 on v0

v1 whole, which is shorter than its diff:
```python
import jax
import jax.numpy as jnp
from jax import lax
from jax.experimental import pallas as pl
from jax.experimental.pallas import tpu as pltpu
from jax.sharding import PartitionSpec as P

H = 16
HD = 64
NB = 32
D = 1024
FF = 2816
WINDOW = 1024
EXPERTS = 16
CAP = 20
TS = 128
FSDP = 8
SHARD = FF // FSDP
TOK = 2 * TS
BUF = EXPERTS * 2 * CAP
SEQ = EXPERTS * TS
EPS = 1e-06
MASKED = -1e30
EDGES = tuple(range(1, 17)) + (19, 21, 24, 27, 31, 35, 40, 46, 52, 59, 67, 77, 87, 99, 113)
GELU_C = 0.7978845608028654
BF = jnp.bfloat16
F32 = jnp.float32
VMEM_LIMIT = 58 * 1024 * 1024


def nn(left, right):
    return lax.dot_general(left, right, (((1,), (0,)), ((), ())), preferred_element_type=F32)


def nt(left, right):
    return lax.dot_general(left, right, (((1,), (1,)), ((), ())), preferred_element_type=F32)


def tn(left, right):
    return lax.dot_general(left, right, (((0,), (0,)), ((), ())), preferred_element_type=F32)


def halves(value):
    high = value.astype(BF)
    return high, (value - high.astype(F32)).astype(BF)


def call(kernel, out_shape, *args, scratch=(), in_specs=None, **kw):
    return pl.pallas_call(
        kernel,
        out_shape=out_shape,
        in_specs=in_specs or [pl.BlockSpec(memory_space=pltpu.VMEM)] * len(args),
        out_specs=jax.tree.map(lambda _: pl.BlockSpec(memory_space=pltpu.VMEM), out_shape),
        scratch_shapes=list(scratch),
        compiler_params=pltpu.CompilerParams(vmem_limit_bytes=VMEM_LIMIT),
        **kw,
    )(*args)


def shape(dims, dtype):
    return jax.ShapeDtypeStruct(dims, dtype)


def lane_half(dims):
    return lax.broadcasted_iota(jnp.int32, dims, 1) % 128 < HD


def pack_pair(first, second):
    left = lane_half(first.shape)
    return (
        jnp.where(left, first, pltpu.roll(second, HD, 1)).astype(BF),
        jnp.where(left, pltpu.roll(first, HD, 1), second).astype(BF),
    )


def qkv_kernel(x_ref, gain_ref, wq_ref, wk_ref, wv_ref, normed_ref, out_ref):
    x = x_ref[...].astype(F32)
    factor = lax.rsqrt(jnp.mean(x * x, axis=-1, keepdims=True) + EPS)
    normed = (x * factor * gain_ref[...]).astype(BF)
    normed_ref[...] = normed
    for which, w_ref in enumerate((wq_ref, wk_ref, wv_ref)):
        for part in range(4):
            res = nn(normed, w_ref[:, part * 256 : (part + 1) * 256])
            for pair in range(2):
                head = part * 4 + pair * 2
                cols = slice(pair * 128, pair * 128 + 128)
                one, two = pack_pair(res[:TS, cols], res[TS:, cols])
                out_ref[head, which * TS : (which + 1) * TS, :] = one
                out_ref[head + 1, which * TS : (which + 1) * TS, :] = two


def attn_setup(len_ref, tab_ref, recv_ref, kext, qext, bias):
    rows = lax.broadcasted_iota(jnp.int32, (SEQ, 128), 0)
    lanes = lax.broadcasted_iota(jnp.int32, (SEQ, 128), 1)
    end1 = [len_ref[m, 0] for m in range(2)]
    end2 = [len_ref[m, 0] + len_ref[m, 1] for m in range(2)]
    kfeat = jnp.where(lanes == 4, 1.0, 0.0)
    for m in range(2):
        kfeat = jnp.where((lanes == 2 * m) & (rows < end1[m]), 1.0, kfeat)
        kfeat = jnp.where((lanes == 2 * m + 1) & (rows < end2[m]), 1.0, kfeat)
    kext[:, 128:] = kfeat.astype(BF)
    for i in range(EXPERTS):
        kext[i * TS : (i + 1) * TS, :128] = recv_ref[i, TS : 2 * TS, :]
    left = lane_half((TS, 128))
    row_in = lax.broadcasted_iota(jnp.int32, (TS, 128), 0)
    lane_in = lax.broadcasted_iota(jnp.int32, (TS, 128), 1)
    for i in range(EXPERTS):
        q2 = recv_ref[i, 0:TS, :].astype(F32) * (HD**-0.5)
        pos = row_in + i * TS
        for m in range(2):
            keep = left if m == 0 else jnp.logical_not(left)
            qext[i, m * TS : (m + 1) * TS, :128] = jnp.where(keep, q2, 0.0).astype(BF)
            feat = jnp.where((lane_in == 2 * m) & (pos >= end1[m]), MASKED, 0.0)
            feat = jnp.where((lane_in == 2 * m + 1) & (pos >= end2[m]), MASKED, feat)
            qext[i, m * TS : (m + 1) * TS, 128:] = feat.astype(BF)
    for block in range(12):
        dist = 1024 - block * TS + lane_in - row_in
        if block in (7, 8):
            value = jnp.full((TS, 128), tab_ref[0, 0], F32)
            for bucket, edge in enumerate(EDGES):
                value = jnp.where(dist >= edge, tab_ref[0, bucket + 1], value)
        else:
            value = jnp.full((TS, 128), tab_ref[0, NB - 1], F32)
        value = jnp.where((dist >= 0) & (dist < WINDOW), value, MASKED)
        bias[block * TS : (block + 1) * TS, :128] = value
        bias[block * TS : (block + 1) * TS, 128:] = value


def eye(size):
    return (
        lax.broadcasted_iota(jnp.int32, (size, size), 0)
        == lax.broadcasted_iota(jnp.int32, (size, size), 1)
    ).astype(BF)


def strip_loops(strip):
    def early(i, carry):
        strip(i, 4, 0)
        return carry

    def middle(i, carry):
        strip(i, 8, 0)
        return carry

    def late(i, carry):
        strip(i, 9, i - 8)
        return carry

    lax.fori_loop(0, 4, early, 0)
    lax.fori_loop(4, 8, middle, 0)
    lax.fori_loop(8, 16, late, 0)


def span(block, count):
    return pl.ds(pl.multiple_of(block * TS, TS), count * TS)


def attn_fwd_kernel(len_ref, tab_ref, recv_ref, out_ref, lse_ref, kext, qext, bias, vt):
    attn_setup(len_ref, tab_ref, recv_ref, kext, qext, bias)
    unit = eye(TS)
    for i in range(EXPERTS):
        vt[:, i * TS : (i + 1) * TS] = nt(unit, recv_ref[i, 2 * TS : 3 * TS, :]).astype(BF)

    def strip(i, count, first):
        s = nt(kext[span(first, count), :], qext[i]) + bias[span(first - i + 8, count), :]
        top = jnp.max(s, axis=0, keepdims=True)
        p = jnp.exp(s - top)
        total = jnp.sum(p, axis=0, keepdims=True)
        res = nn(vt[:, span(first, count)], p.astype(BF)) / total
        both = jnp.concatenate([res[:HD, :TS], res[HD:, TS:]], axis=0)
        out_ref[i] = both.T.astype(BF)
        lse_ref[i] = jnp.broadcast_to(top + jnp.log(total), (8, TOK))

    strip_loops(strip)


def attn_bwd_kernel(
    len_ref, tab_ref, recv_ref, dout_ref, lse_ref, out_ref, tab_out_ref, kext, qext, bias, ktext, dk, dv, near, far
):
    attn_setup(len_ref, tab_ref, recv_ref, kext, qext, bias)
    unit = eye(256)
    for i in range(EXPERTS):
        ktext[:, i * TS : (i + 1) * TS] = nt(unit, kext[i * TS : (i + 1) * TS, :])[:144].astype(BF)
    dk[...] = jnp.zeros_like(dk)
    dv[...] = jnp.zeros_like(dv)
    near[...] = jnp.zeros_like(near)
    far[...] = jnp.zeros_like(far)
    left = lane_half((TS, 128))

    def strip(i, count, first):
        q = qext[i]
        s = nt(kext[span(first, count), :], q) + bias[span(first - i + 8, count), :]
        p = jnp.exp(s - lse_ref[i][0:1])
        do2 = dout_ref[i]
        zero = jnp.zeros_like(do2)
        do = jnp.concatenate([jnp.where(left, do2, zero), jnp.where(left, zero, do2)], axis=0)
        if count == 9:
            v = recv_ref[pl.ds(first, count), 2 * TS : 3 * TS, :].reshape(count * TS, 128)
        else:
            v = recv_ref[0:count, 2 * TS : 3 * TS, :].reshape(count * TS, 128)
        dp = nt(v, do)
        inner = jnp.sum(p * dp, axis=0, keepdims=True)
        ds = (p * (dp - inner)).astype(BF)
        dv[span(first, count), :] += nn(p.astype(BF), do)
        dk[span(first, count), :] += nn(ds, q[:, :128])
        dqt = nn(ktext[:, span(first, count)], ds)
        both = jnp.concatenate([dqt[:HD, :TS], dqt[HD : 2 * HD, TS:]], axis=0) * (HD**-0.5)
        out_ref[i, 0:TS, :] = both.T.astype(BF)
        far[...] += dqt[128:136]
        if count == 9:
            near[...] += ds[7 * TS :].astype(F32)
        else:
            nearby.append(ds)

    nearby = []

    def loop(low, high, count):
        def body(i, carry):
            nearby.clear()
            first = i - 8 if count == 9 else 0
            strip(i, count, first)
            if count != 9:
                ds = nearby[0]
                for block in range(count):
                    value = ds[block * TS : (block + 1) * TS].astype(F32)

                    @pl.when(i == block)
                    def _(value=value):
                        near[TS:] += value

                    @pl.when(i == block + 1)
                    def _(value=value):
                        near[:TS] += value

            return carry

        lax.fori_loop(low, high, body, 0)

    loop(0, 4, 4)
    loop(4, 8, 8)
    loop(8, 16, 9)
    for i in range(EXPERTS):
        out_ref[i, TS : 2 * TS, :] = dk[i * TS : (i + 1) * TS, :].astype(BF)
        out_ref[i, 2 * TS :, :] = dv[i * TS : (i + 1) * TS, :].astype(BF)
    grads = near[:, :TS] + near[:, TS:]
    dist = (
        TS
        + lax.broadcasted_iota(jnp.int32, (TOK, TS), 1)
        - lax.broadcasted_iota(jnp.int32, (TOK, TS), 0)
    )
    total = jnp.sum(far[4:5, :])
    lane = lax.broadcasted_iota(jnp.int32, (8, 128), 1)
    res = jnp.zeros((8, 128), F32)
    lows = (0,) + EDGES
    seen = 0.0
    for b in range(NB - 1):
        part = jnp.sum(jnp.where((dist >= lows[b]) & (dist < lows[b + 1]), grads, 0.0))
        seen = seen + part
        res = jnp.where(lane == b, part, res)
    res = jnp.where(lane == NB - 1, total - seen, res)
    tab_out_ref[...] = res


def row_expert():
    row = lax.broadcasted_iota(jnp.int32, (BUF, 128), 0)
    lane = lax.broadcasted_iota(jnp.int32, (BUF, 128), 1) * (2 * CAP)
    return (row >= lane) & (row < lane + 2 * CAP)


def unpack_heads(recv_ref, lo, emit):
    for pair in range(H // 2):
        one = recv_ref[2 * pair, lo : lo + TS, :].astype(F32)
        two = recv_ref[2 * pair + 1, lo : lo + TS, :].astype(F32)
        first, second = pack_pair(one, two)
        emit(pair, first, second)


def slot_share(place, share_e, own):
    high, low = halves(share_e)
    return jnp.sum(jnp.where(own, nn(place, high) + nn(place, low), 0.0), axis=1, keepdims=True)


def mid_kernel(
    recv_ref, x_ref, wo_ref, gain_ref, wr_ref, mask_ref, place_ref, dy_ref,
    att_ref, hidden_ref, mixed_ref, share_ref, send_ref,
):
    def emit(pair, first, second):
        att_ref[0:TS, pair * 128 : pair * 128 + 128] = first
        att_ref[TS:, pair * 128 : pair * 128 + 128] = second

    unpack_heads(recv_ref, 0, emit)
    hidden = x_ref[...].astype(F32) + nn(att_ref[...], wo_ref[...])
    hidden_ref[...] = hidden
    factor = lax.rsqrt(jnp.mean(hidden * hidden, axis=-1, keepdims=True) + EPS)
    mixed = (hidden * factor * gain_ref[...]).astype(BF)
    mixed_ref[...] = mixed
    place = place_ref[...]
    send_ref[:, :D] = nn(place, mixed).astype(BF)
    picked = mask_ref[...] > 0
    logits = jnp.where(picked, nn(mixed, wr_ref[...]), MASKED)
    weight = jnp.exp(logits - jnp.max(logits, axis=1, keepdims=True))
    share = weight / jnp.sum(weight, axis=1, keepdims=True)
    share_ref[...] = share
    send_ref[:, D:] = (slot_share(place, share, row_expert()) * nn(place, dy_ref[...])).astype(BF)


def expert_kernel(rows_ref, w_ref, out_ref, grad_ref, acc_out, acc_row):
    step = pl.program_id(0)

    @pl.when(step == 0)
    def _():
        acc_out[...] = jnp.zeros_like(acc_out)
        acc_row[...] = jnp.zeros_like(acc_row)

    rows = rows_ref[:, :D]
    slot_grad = rows_ref[:, D:]
    gate_w = w_ref[:, 0:SHARD, :].reshape(2 * SHARD, D)
    up_w = w_ref[:, SHARD : 2 * SHARD, :].reshape(2 * SHARD, D)
    down_w = w_ref[:, 2 * SHARD :, :].reshape(2 * SHARD, D)
    gate = nt(rows, gate_w)
    up = nt(rows, up_w)
    act_grad = nt(slot_grad, down_w).astype(BF).astype(F32)
    square = gate * gate
    tanh = jnp.tanh(GELU_C * gate * (1.0 + 0.044715 * square))
    gelu = 0.5 * gate * (1.0 + tanh)
    slope = 0.5 * (1.0 + tanh) + 0.5 * gate * (1.0 - tanh * tanh) * (
        GELU_C * (1.0 + 3 * 0.044715 * square)
    )
    act = (gelu * up).astype(BF)
    gate_grad = (act_grad * up * slope).astype(BF)
    up_grad = (act_grad * gelu).astype(BF)
    acc_out[...] += nn(act, down_w)
    acc_row[...] += nn(gate_grad, gate_w) + nn(up_grad, up_w)
    grad_ref[:, 0:SHARD, :] = tn(gate_grad, rows).astype(BF).reshape(2, SHARD, D)
    grad_ref[:, SHARD : 2 * SHARD, :] = tn(up_grad, rows).astype(BF).reshape(2, SHARD, D)
    grad_ref[:, 2 * SHARD :, :] = tn(act, slot_grad).astype(BF).reshape(2, SHARD, D)

    @pl.when(step == pl.num_programs(0) - 1)
    def _():
        out_ref[:, :D] = acc_out[...].astype(BF)
        out_ref[:, D:] = acc_row[...].astype(BF)


def back_kernel(
    ret_ref, place_ref, place_t_ref, dy_ref, hidden_ref, mixed_ref, share_ref, wr_ref, gain_ref, wo_ref,
    result_ref, hgrad_ref, branch_ref, send_ref, router_ref, gain_out_ref,
):
    place = place_ref[...]
    place_t = place_t_ref[...]
    own = row_expert()
    dy = dy_ref[...]
    returned = ret_ref[:, :D]
    dots = jnp.sum(nn(place, dy) * returned.astype(F32), axis=1, keepdims=True)
    high, low = halves(jnp.where(own, dots, 0.0))
    share = share_ref[...]
    share_grad = nn(place_t, high) + nn(place_t, low)
    inner = jnp.sum(share * share_grad, axis=1, keepdims=True)
    lg_high, lg_low = halves(share * (share_grad - inner))
    wr = wr_ref[...]
    mixed_grad = nn(place_t, ret_ref[:, D:]) + (nt(lg_high, wr) + nt(lg_low, wr))
    hidden = hidden_ref[...]
    factor = lax.rsqrt(jnp.mean(hidden * hidden, axis=-1, keepdims=True) + EPS)
    unit = hidden * factor
    gain_out_ref[...] = jnp.broadcast_to(jnp.sum(mixed_grad * unit, axis=0, keepdims=True), (8, D))
    scaled = mixed_grad * gain_ref[...]
    hgrad = dy.astype(F32) + factor * (
        scaled - unit * jnp.mean(scaled * unit, axis=-1, keepdims=True)
    )
    hgrad_ref[...] = hgrad
    branch = hgrad.astype(BF)
    branch_ref[...] = branch
    for part in range(4):
        res = nt(branch, wo_ref[part * 256 : (part + 1) * 256, :])
        for pair in range(2):
            head = part * 4 + pair * 2
            cols = slice(pair * 128, pair * 128 + 128)
            one, two = pack_pair(res[:TS, cols], res[TS:, cols])
            send_ref[head] = one
            send_ref[head + 1] = two
    mixed = mixed_ref[...]
    router_ref[...] = tn(mixed, lg_high) + tn(mixed, lg_low)
    scale_high, scale_low = halves(
        place_t.astype(F32) * slot_share(place, share, own).T
    )
    moe = nn(scale_high, returned) + nn(scale_low, returned)
    result_ref[...] = (hidden + moe).astype(BF)


def final_kernel(
    recv_ref, normed_ref, x_ref, gain_ref, hgrad_ref, wq_ref, wk_ref, wv_ref,
    igrad_ref, gq_ref, gk_ref, gv_ref, gain_out_ref, flat,
):
    normed = normed_ref[...]
    total = None
    for which, (w_ref, g_ref) in enumerate(((wq_ref, gq_ref), (wk_ref, gk_ref), (wv_ref, gv_ref))):

        def emit(pair, first, second):
            flat[0:TS, pair * 128 : pair * 128 + 128] = first
            flat[TS:, pair * 128 : pair * 128 + 128] = second

        unpack_heads(recv_ref, which * TS, emit)
        grad = flat[...]
        g_ref[...] = tn(normed, grad).astype(BF)
        part = nt(grad, w_ref[...])
        total = part if total is None else total + part
    x = x_ref[...].astype(F32)
    factor = lax.rsqrt(jnp.mean(x * x, axis=-1, keepdims=True) + EPS)
    unit = x * factor
    gain_out_ref[...] = jnp.broadcast_to(jnp.sum(total * unit, axis=0, keepdims=True), (8, D))
    scaled = total * gain_ref[...]
    igrad_ref[...] = (
        hgrad_ref[...]
        + factor * (scaled - unit * jnp.mean(scaled * unit, axis=-1, keepdims=True))
    ).astype(BF)


def exchanged(payload):
    return lax.all_to_all(payload, "expert", split_axis=0, concat_axis=0, tiled=True)


def placement(routes, order):
    micro = routes.shape[0]
    slots = routes.reshape(micro, 2 * TS)
    rank_of = order.reshape(micro, 2 * TS)
    same = slots[:, :, None] == slots[:, None, :]
    earlier = rank_of[:, None, :] < rank_of[:, :, None]
    rank = jnp.sum((same & earlier).astype(jnp.int32), axis=2)
    base = slots * (2 * CAP) + jnp.arange(micro, dtype=jnp.int32)[:, None] * CAP
    target = jnp.where(rank < CAP, base + rank, BUF).reshape(micro * TS, 2)
    rows = jnp.arange(BUF, dtype=jnp.int32)
    place = (rows[:, None] == target[None, :, 0]) | (rows[:, None] == target[None, :, 1])
    place_t = (rows[None, :] == target[:, 0:1]) | (rows[None, :] == target[:, 1:2])
    return place.astype(BF), place_t.astype(BF)


def on_device(
    tokens, cotangent, doc_lengths, routes, order, gain_attn, w_query, w_key, w_value, w_out,
    rel_table, gain_moe, w_router, w_gate, w_up, w_down,
):
    expert_shard = jnp.concatenate([w_gate[0].T, w_up[0].T, w_down[0]], axis=0)
    extra = jnp.zeros((8, 128), BF)
    extra = extra.at[:, :EXPERTS].set(w_router).at[:, 16].set(gain_attn).at[:, 17].set(gain_moe)
    shared = jnp.concatenate(
        [
            jnp.concatenate([w_query, w_key, w_value, w_out], axis=0),
            jnp.pad(extra, ((0, 24), (0, 0))),
        ],
        axis=1,
    )
    near_by = lax.all_gather(shared, "expert", axis=0, tiled=False)
    everyone = lax.all_gather(near_by, "fsdp", axis=1, tiled=False)
    table = lax.all_gather(rel_table, "fsdp", axis=0, tiled=True).astype(F32).reshape(1, NB)
    expert_w = lax.all_gather(expert_shard, "fsdp", axis=0, tiled=False)
    wq, wk, wv, wo = (
        everyone[:, :, 8 * k : 8 * k + 8, :D].reshape(D, D) for k in range(4)
    )
    small = everyone[:, :, 0:8, D:].reshape(D, 128)
    wr = jnp.where(jnp.arange(128) < EXPERTS, small, 0).astype(BF)
    attn_gain = small[:, 16].astype(F32).reshape(1, D)
    moe_gain = small[:, 17].astype(F32).reshape(1, D)
    place, place_t = placement(routes[:, 0], order[:, 0, 0])
    lanes = jnp.arange(128, dtype=jnp.int32)
    route_rows = routes.reshape(TOK, 2)
    picked = (
        (route_rows[:, 0:1] == lanes) | (route_rows[:, 1:2] == lanes)
    ).astype(F32)
    x = tokens.reshape(TOK, D)
    dy = cotangent.reshape(TOK, D)
    lengths = doc_lengths[:, 0]

    normed, packed = call(
        qkv_kernel,
        (shape((TOK, D), BF), shape((H, 3 * TS, 128), BF)),
        x, attn_gain, wq, wk, wv,
    )
    heads = exchanged(packed)
    smem = pl.BlockSpec(memory_space=pltpu.SMEM)
    vmem = pl.BlockSpec(memory_space=pltpu.VMEM)
    attn_scratch = [
        pltpu.VMEM((SEQ, 256), BF),
        pltpu.VMEM((EXPERTS, TOK, 256), BF),
        pltpu.VMEM((12 * TS, TOK), F32),
    ]
    attended, lse = call(
        attn_fwd_kernel,
        (shape((EXPERTS, TS, 128), BF), shape((EXPERTS, 8, TOK), F32)),
        lengths, table, heads,
        in_specs=[smem, smem, vmem],
        scratch=attn_scratch + [pltpu.VMEM((128, SEQ), BF)],
    )
    att_back = exchanged(attended)
    att, hidden, mixed, share, send = call(
        mid_kernel,
        (
            shape((TOK, D), BF), shape((TOK, D), F32), shape((TOK, D), BF),
            shape((TOK, 128), F32), shape((BUF, 2 * D), BF),
        ),
        att_back, x, wo, moe_gain, wr, picked, place, dy,
    )
    received = exchanged(send.reshape(EXPERTS, 2 * CAP, 2 * D)).reshape(BUF, 2 * D)
    expert_out, expert_grads = pl.pallas_call(
        expert_kernel,
        grid=(FSDP // 2,),
        out_shape=(shape((BUF, 2 * D), BF), shape((FSDP, 3 * SHARD, D), BF)),
        in_specs=[
            pl.BlockSpec((BUF, 2 * D), lambda i: (0, 0)),
            pl.BlockSpec((2, 3 * SHARD, D), lambda i: (i, 0, 0)),
        ],
        out_specs=(
            pl.BlockSpec((BUF, 2 * D), lambda i: (0, 0)),
            pl.BlockSpec((2, 3 * SHARD, D), lambda i: (i, 0, 0)),
        ),
        scratch_shapes=[pltpu.VMEM((BUF, D), F32), pltpu.VMEM((BUF, D), F32)],
        compiler_params=pltpu.CompilerParams(vmem_limit_bytes=VMEM_LIMIT),
    )(received, expert_w)
    expert_sum = lax.psum_scatter(
        expert_grads.reshape(FSDP * 3 * SHARD, D), "fsdp", scatter_dimension=0, tiled=True
    ).astype(F32)
    returned = exchanged(expert_out.reshape(EXPERTS, 2 * CAP, 2 * D)).reshape(BUF, 2 * D)
    result, hgrad, branch, att_grad, router_grad, moe_gain_grad = call(
        back_kernel,
        (
            shape((TOK, D), BF), shape((TOK, D), F32), shape((TOK, D), BF),
            shape((H, TS, 128), BF), shape((D, 128), F32), shape((8, D), F32),
        ),
        returned, place, place_t, dy, hidden, mixed, share, wr, moe_gain, wo,
    )
    out_grad = tn(att, branch).astype(BF)
    head_grads = exchanged(att_grad)
    qkv_grads, table_grad = call(
        attn_bwd_kernel,
        (shape((EXPERTS, 3 * TS, 128), BF), shape((8, 128), F32)),
        lengths, table, heads, head_grads, lse,
        in_specs=[smem, smem, vmem, vmem, vmem],
        scratch=attn_scratch
        + [
            pltpu.VMEM((144, SEQ), BF),
            pltpu.VMEM((SEQ, 128), F32),
            pltpu.VMEM((SEQ, 128), F32),
            pltpu.VMEM((2 * TS, TOK), F32),
            pltpu.VMEM((8, TOK), F32),
        ],
    )
    token_grads = exchanged(qkv_grads)
    input_grad, gq, gk, gv, attn_gain_grad = call(
        final_kernel,
        (
            shape((TOK, D), BF), shape((D, D), BF), shape((D, D), BF), shape((D, D), BF),
            shape((8, D), F32),
        ),
        token_grads, normed, x, attn_gain, hgrad, wq, wk, wv,
        scratch=[pltpu.VMEM((TOK, D), BF)],
    )
    small_grad = jnp.concatenate(
        [
            router_grad[:, :EXPERTS],
            attn_gain_grad[0][:, None],
            moe_gain_grad[0][:, None],
        ],
        axis=1,
    ).astype(BF)
    small_grad = jnp.pad(small_grad, ((0, 0), (0, 110))).reshape(EXPERTS * FSDP, 8, 128)
    grads = jnp.concatenate(
        [
            jnp.concatenate([g.reshape(EXPERTS * FSDP, 8, D) for g in (gq, gk, gv, out_grad)], axis=1),
            jnp.pad(small_grad, ((0, 0), (0, 24), (0, 0))),
        ],
        axis=2,
    )
    grads = grads.reshape(EXPERTS, FSDP, 32, D + 128).swapaxes(0, 1)
    grads = lax.psum_scatter(grads, "fsdp", scatter_dimension=0, tiled=False)
    grads = lax.psum_scatter(grads, "expert", scatter_dimension=0, tiled=False).astype(F32)
    table_out = lax.psum_scatter(table_grad[0, :NB], "fsdp", scatter_dimension=0, tiled=True)
    return (
        result.reshape(tokens.shape),
        input_grad.reshape(tokens.shape),
        grads[0:8, D + 16],
        grads[0:8, :D],
        grads[8:16, :D],
        grads[16:24, :D],
        grads[24:32, :D],
        table_out,
        grads[0:8, D + 17],
        grads[0:8, D : D + EXPERTS],
        expert_sum[:SHARD].T[None],
        expert_sum[SHARD : 2 * SHARD].T[None],
        expert_sum[2 * SHARD :][None],
    )


def solution(mesh):
    row = P(None, "fsdp", "expert", None)
    flat = P(("expert", "fsdp"))
    matrix = P(("expert", "fsdp"), None)
    columns = P("expert", None, "fsdp")
    deep = P("expert", "fsdp", None)
    return jax.shard_map(
        on_device,
        mesh=mesh,
        in_specs=(
            row, row, P(None, "fsdp", None), row, row, flat, matrix, matrix, matrix, matrix,
            flat, flat, matrix, columns, columns, deep,
        ),
        out_specs=(
            row, row, flat, matrix, matrix, matrix, matrix, flat, flat, matrix, columns, columns, deep,
        ),
        check_vma=False,
    )
```

time: 4170 us -> 715 us (0.17)
  waiting for transfers between devices: 3150 us -> 431 us
  local copies, waits for them, and re-layouts: 469 us -> 23.3 us
  matrix products: 261 us -> 0.74 us
  Pallas kernels: 0 us -> 118 us
  blocking collectives: 169 us -> 80 us
    reduce_scatter x6 -> x1, waiting for transfers between devices: 2640 us -> 93.9 us  [on_device(): lax.psum_scatter(expert_grads.reshape(FSDP * 3 * SHARD, D), 'fsdp', scatt...]
    unnamed x340 -> x29, local copies, waits for them, and re-layouts: 336 us -> 6.03 us
    dot_general x71 -> x1, matrix products: 261 us -> 0.74 us  [tn(): lax.dot_general(left, right, (((0,), (0,)), ((), ())), preferred_element_...]
    all_gather x11 -> x3, waiting for transfers between devices: 341 us -> 98.5 us  [the longest x1 52.8 us: on_device(): everyone = lax.all_gather(near_by, 'fsdp', axis=1, tiled=False)]
    pallas_call x0 -> x7, Pallas kernels: none -> 118 us  [the longest x6 71.3 us: call(): pl.pallas_call(kernel, out_shape=out_shape, in_specs=in_specs or [pl.Bloc...]
    unnamed x2, blocking collectives: 135 us -> 25.6 us
    dynamic_update_slice x4 -> x0, local copies, waits for them, and re-layouts: 77 us -> none  [the longest x2 38.9 us: on_device(): lax.dynamic_update_slice_in_dim(zero_rows, key_part, key_start, 1)]
    all_to_all x0 -> x2, blocking collectives: none -> 54.4 us  [exchanged(): lax.all_to_all(payload, 'expert', split_axis=0, concat_axis=0, tiled=True)]
  transfers between devices with their start and end apart: 34 -> 10, of which waited for: 25 -> 9; matrix products, arithmetic and copies ran while one was open for 15% -> 3% of each run, Pallas kernels for 0% -> 4%
where the time goes in v1:
time: 715 us; the launch traced here: 713 us
  waiting for transfers between devices  431 us (60%)
  Pallas kernels  118 us (17%)
  blocking collectives  80 us (11%)
  other arithmetic  25.4 us (4%)
  local copies, waits for them, and re-layouts  23.3 us (3%)
  starting transfers between devices  19.3 us (3%)
  between operations  15.7 us (2%)
    unnamed x8, waiting for transfers between devices  172 us
    reduce_scatter x1, waiting for transfers between devices, on_device(): lax.psum_scatter(expert_grads.reshape(FSDP * 3 * SHARD, D), 'fsdp', scatt...  93.9 us
    pallas_call x6, Pallas kernels, call(): pl.pallas_call(kernel, out_shape=out_shape, in_specs=in_specs or [pl.Bloc...  71.3 us
    all_to_all x4, waiting for transfers between devices, exchanged(): lax.all_to_all(payload, 'expert', split_axis=0, concat_axis=0, tiled=True)  66.6 us
    all_to_all x2, blocking collectives, exchanged(): lax.all_to_all(payload, 'expert', split_axis=0, concat_axis=0, tiled=True)  54.4 us
    all_gather x1, waiting for transfers between devices, on_device(): everyone = lax.all_gather(near_by, 'fsdp', axis=1, tiled=False)  52.8 us
    pallas_call x1, Pallas kernels, on_device(): pl.pallas_call(expert_kernel, grid=(FSDP // 2,), out_shape=(shape((BUF, 2...  46.8 us
    all_gather x1, waiting for transfers between devices, on_device(): near_by = lax.all_gather(shared, 'expert', axis=0, tiled=False)  45.7 us
  transfers between devices with their start and end apart: 10, of which 9 were waited for; matrix products, arithmetic and copies ran while one was open for 3% of the time, Pallas kernels for 4%

profile of v1, /device:TPU:1, one launch (start us, length us, event | category | flops | bytes accessed | tf_op | source)
XLA Modules:
  0.0 713.3 jit_solution(14022794768722885144)
XLA Ops:
  14.8 45.7 %all-gather.7.cloned.1.call-done = bf16[512,1152]{1,0:T(8,128)(2,1)} async-done(((bf16[32,1152]{1,0:T(8,128)(2,1)}), bf16[512,1152]{1,0:T(8,128)(2,1)}) %all-gather.7.cloned.1.call-update) | async-done | bytes 1179664 | tf_op jit(solution)/shard_map/all_gather | solution.py:450
  64.0 52.8 %all-gather.9.cloned.1.call-done = bf16[16,256,1152]{2,1,0:T(8,128)(2,1)} async-done(((bf16[16,32,1152]{2,1,0:T(8,128)(2,1)}), bf16[16,256,1152]{2,1,0:T(8,128)(2,1)}) %all-gather.9.cloned.1.call-update) | async-done | bytes 9437200 | tf_op jit(solution)/shard_map/all_gather | solution.py:451
  118.7 6.2 fusion.13
  124.9 6.5 shard_map.255
  131.5 6.7 all-to-all-start
  140.3 12.8 %all-reduce.4 = bf16[32]{0:T(256)(128)(2,1)S(1)} all-reduce(bf16[32]{0:T(256)(128)(2,1)S(1)} %dynamic-update-slice.9), channel_id=1, replica_groups=mesh['expert'=16,'fsdp'=8] {'fsdp'}, use_global_device_ids=true, to_apply=%add.4 | all-reduce | flops 32 | bytes 128
  154.5 8.3 %all-to-all-done.recv_ref = bf16[16,384,128]{2,1,0:T(8,128)(2,1)S(1)} async-done(((bf16[16,384,128]{2,1,0:T(8,128)(2,1)}), bf16[16,384,128]{2,1,0:T(8,128)(2,1)S(1)}, u32[]{:S(2)}, u32[]{:S(2)}) %all-to-all-start) | async-done | bytes 1572896 | tf_op jit(solution)/shard_map/all_to_all | solution.py:418
  164.0 18.4 %shard_map.256 = (bf16[16,128,128]{2,1,0:T(8,128)(2,1)}, f32[16,8,256]{2,1,0:T(8,128)}) custom-call(s32[2,3]{1,0:T(2,128)} %bitcast.136, f32[1,32]{1,0:T(1,128)} %bitcast_convert_fusion.1.tab_ref, bf16[16,384,128]{2,1,0:T(8,128)(2,1)} %copy-done), custom_call_target="tpu_custom_call" | custom-call | tf_op jit(solution)/shard_map/pallas_call | solution.py:49
  187.7 8.8 %all-to-all-done.1.recv_ref = bf16[16,128,128]{2,1,0:T(8,128)(2,1)S(1)} async-done(((bf16[16,128,128]{2,1,0:T(8,128)(2,1)}), bf16[16,128,128]{2,1,0:T(8,128)(2,1)S(1)}, u32[]{:S(2)}, u32[]{:S(2)}) %all-to-all-start.1) | async-done | bytes 524320 | tf_op jit(solution)/shard_map/all_to_all | solution.py:418
  197.4 6.2 shard_map.257
  203.6 36.9 %all_to_all.30 = bf16[16,40,2048]{2,1,0:T(8,128)(2,1)} all-to-all(bf16[16,40,2048]{2,1,0:T(8,128)(2,1)} %bitcast.116), channel_id=1, replica_groups=mesh['expert'=16,'fsdp'=8] {'expert'}, dimensions={0} | all-to-all | bytes 5242880 | tf_op jit(solution)/shard_map/all_to_all | solution.py:418
  240.5 46.8 %shard_map.258 = (bf16[640,2048]{1,0:T(8,128)(2,1)}, bf16[8,1056,1024]{2,1,0:T(8,128)(2,1)}) custom-call(bf16[640,2048]{1,0:T(8,128)(2,1)} %bitcast.108, bf16[8,1056,1024]{2,1,0:T(8,128)(2,1)} %bitcast.105), custom_call_target="tpu_custom_call" | custom-call | tf_op jit(solution)/shard_map/pallas_call | solution.py:501
  292.2 31.5 %all-to-all-done.3 = bf16[16,40,2048]{2,1,0:T(8,128)(2,1)S(1)} async-done(((bf16[16,40,2048]{2,1,0:T(8,128)(2,1)}), bf16[16,40,2048]{2,1,0:T(8,128)(2,1)S(1)}, u32[]{:S(2)}, u32[]{:S(2)}) %all-to-all-start.3) | async-done | bytes 2621472 | tf_op jit(solution)/shard_map/all_to_all | solution.py:418
  325.2 8.3 %shard_map.259 = (bf16[256,1024]{1,0:T(8,128)(2,1)}, f32[256,1024]{1,0:T(8,128)}, bf16[256,1024]{1,0:T(8,128)(2,1)}, bf16[16,128,128]{2,1,0:T(8,128)(2,1)}, f32[1024,128]{1,0:T(8,128)}, /*index=5*/f32[8,1024]{1,0:T(8,128)}) custom-call(bf16[640,2048]{1,0:T(8,128)(2,1)} %bitcast.107, bf16[640,256]{1,0:T(8,128)(2,1)} %fusion.3.place_ref, ...), custom_call_target="tpu_custom_call" | custom-call | tf_op jit(solution)/shard_map/pallas_call | solution.py:49
  333.5 17.5 %all_to_all.31.dout_ref = bf16[16,128,128]{2,1,0:T(8,128)(2,1)} all-to-all(bf16[16,128,128]{2,1,0:T(8,128)(2,1)} %get-tuple-element.81), channel_id=1, replica_groups=mesh['expert'=16,'fsdp'=8] {'expert'}, dimensions={0} | all-to-all | bytes 1048576 | tf_op jit(solution)/shard_map/all_to_all | solution.py:418
  350.9 23.0 %shard_map.260 = (bf16[16,384,128]{2,1,0:T(8,128)(2,1)}, f32[8,128]{1,0:T(8,128)}) custom-call(s32[2,3]{1,0:T(2,128)} %bitcast.137, f32[1,32]{1,0:T(1,128)} %bitcast_convert_fusion.1.tab_ref, bf16[16,384,128]{2,1,0:T(8,128)(2,1)} %copy-done, bf16[16,128,128]{2,1,0:T(8,128)(2,1)} %all_to_all.31.dout_ref, f32[16,8,256]{2,1,0:T(8,128)} %get-tuple-element.82.lse_ref), custom_call_target="tpu_custom_call" | custom-call | tf_op jit(solution)/shard_map/pallas_call | solution.py:49
  374.0 4.4 all-to-all-start.5
  380.4 17.9 %all-to-all-done.5.recv_ref = bf16[16,384,128]{2,1,0:T(8,128)(2,1)} async-done(((bf16[16,384,128]{2,1,0:T(8,128)(2,1)}), bf16[16,384,128]{2,1,0:T(8,128)(2,1)}, u32[]{:S(2)}, u32[]{:S(2)}) %all-to-all-start.5) | async-done | bytes 1572896 | tf_op jit(solution)/shard_map/all_to_all | solution.py:418
  398.3 8.8 %shard_map.261 = (bf16[256,1024]{1,0:T(8,128)(2,1)}, bf16[1024,1024]{1,0:T(8,128)(2,1)}, bf16[1024,1024]{1,0:T(8,128)(2,1)}, bf16[1024,1024]{1,0:T(8,128)(2,1)}, f32[8,1024]{1,0:T(8,128)}) custom-call(bf16[16,384,128]{2,1,0:T(8,128)(2,1)} %all-to-all-done.5.recv_ref, bf16[256,1024]{1,0:T(8,128)(2,1)} %get-tuple-element.84.normed_ref, ...), custom_call_target="tpu_custom_call" | custom-call | tf_op jit(solution)/shard_map/pallas_call | solution.py:49
  408.1 7.6 %fusion.1 = bf16[128,32,1152]{2,1,0:T(8,128)(2,1)} fusion(bf16[128,8,128]{2,1,0:T(8,128)(2,1)S(1)} %pad_bitcast_fusion, bf16[128,8,1024]{2,1,0:T(8,128)(2,1)S(1)} %convert_bitcast_fusion, bf16[128,8,1024]{2,1,0:T(8,128)(2,1)} %bitcast.119, bf16[128,8,1024]{2,1,0:T(8,128)(2,1)} %bitcast.118, bf16[128,8,1024]{2,1,0:T(8,128)(2,1)} %bitcast.117), kind=kLoop, calls=%fused_computation.2 | loop fusion | flops 56623104 | bytes 18087936 | tf_op jit(solution)/shard_map/concatenate | solution.py:563
  415.8 114.1 %all-reduce.10.cloned.1.call-done = bf16[8,16,32,1152]{3,2,0,1:T(8,128)(2,1)} async-done(((bf16[8,16,32,1152]{3,2,0,1:T(8,128)(2,1)}), bf16[8,16,32,1152]{3,2,0,1:T(8,128)(2,1)}) %all-reduce.10.cloned.1.call-update) | async-done | bytes 9437200
  534.8 12.8 %all-reduce.7 = f32[32]{0:T(128)S(1)} all-reduce(f32[32]{0:T(128)S(1)} %slice_bitcast_fusion.3), channel_id=7, replica_groups=mesh['expert'=16,'fsdp'=8] {'fsdp'}, use_global_device_ids=true, to_apply=%region_6.7.clone | all-reduce | flops 32 | bytes 256
  548.2 57.3 %reduce-scatter.10.cloned.1.call-done = bf16[1,32,1152]{2,1,0:T(8,128)(2,1)} async-done(((bf16[16,32,1152]{2,1,0:T(8,128)(2,1)}), bf16[1,32,1152]{2,1,0:T(8,128)(2,1)}) %reduce-scatter.10.cloned.1.call-update) | async-done | bytes 73744
  608.4 93.9 %reduce-scatter.8.cloned.1.call-done = bf16[1056,1024]{1,0:T(8,128)(2,1)} async-done(((bf16[8448,1024]{1,0:T(8,128)(2,1)}), bf16[1056,1024]{1,0:T(8,128)(2,1)}) %reduce-scatter.8.cloned.1.call-update) | async-done | bytes 2162704 | tf_op jit(solution)/shard_map/reduce_scatter | solution.py:516
  (87 shorter events, 44.4 us)
Async XLA Ops:
  7.2 53.3 %all-gather.7.cloned.1.call-start = ((), (), s32[]{:S(2)}) async-start(), calls=%async_computation.9 | async-start | bytes 1253376 | tf_op jit(solution)/shard_map/all_gather | solution.py:450
  14.8 102.0 %all-gather.9.cloned.1.call-start = ((), (), s32[]{:S(2)}) async-start(), calls=%async_computation.10 | async-start | bytes 10616832 | tf_op jit(solution)/shard_map/all_gather | solution.py:451
  60.5 180.0 %all-gather.11.cloned.1.call-start = ((), (), s32[]{:S(2)}) async-start(), calls=%async_computation.11 | async-start | bytes 19464192 | tf_op jit(solution)/shard_map/all_gather | solution.py:453
  60.6 3.1 copy-start.6
  60.6 3.4 copy-start.8
  131.5 7.3 %copy-start.7 = (u32[128]{0:T(128)S(1)}, u32[128]{0:T(128)}, u32[]{:S(2)}) copy-start(u32[128]{0:T(128)} %constant.121) | copy-start | bytes 1540
  131.5 8.6 %copy-start.9 = (bf16[4]{0:T(256)(128)(2,1)S(1)}, bf16[4]{0:T(256)(128)(2,1)}, u32[]{:S(2)}) copy-start(bf16[4]{0:T(256)(128)(2,1)} %param.32) | copy-start | bytes 28
  131.5 31.4 %all-to-all-start = ((bf16[16,384,128]{2,1,0:T(8,128)(2,1)}), bf16[16,384,128]{2,1,0:T(8,128)(2,1)S(1)}, u32[]{:S(2)}, u32[]{:S(2)}) async-start(bf16[16,384,128]{2,1,0:T(8,128)(2,1)} %get-tuple-element.73), calls=%async_computation | async-start | bytes 3145728 | tf_op jit(solution)/shard_map/all_to_all | solution.py:418
  162.9 1.2 copy-start
  182.4 14.2 %all-to-all-start.1 = ((bf16[16,128,128]{2,1,0:T(8,128)(2,1)}), bf16[16,128,128]{2,1,0:T(8,128)(2,1)S(1)}, u32[]{:S(2)}, u32[]{:S(2)}) async-start(bf16[16,128,128]{2,1,0:T(8,128)(2,1)} %get-tuple-element.74), calls=%async_computation.1 | async-start | bytes 1048576 | tf_op jit(solution)/shard_map/all_to_all | solution.py:418
  196.6 0.8 copy-start.2
  287.3 36.4 %all-to-all-start.3 = ((bf16[16,40,2048]{2,1,0:T(8,128)(2,1)}), bf16[16,40,2048]{2,1,0:T(8,128)(2,1)S(1)}, u32[]{:S(2)}, u32[]{:S(2)}) async-start(bf16[16,40,2048]{2,1,0:T(8,128)(2,1)} %bitcast.115), calls=%async_computation.3 | async-start | bytes 5242880 | tf_op jit(solution)/shard_map/all_to_all | solution.py:418
  323.7 1.5 copy-start.1
  350.9 27.8 %copy-start.5 = (f32[1024,128]{1,0:T(8,128)S(1)}, f32[1024,128]{1,0:T(8,128)}, u32[]{:S(2)}) copy-start(f32[1024,128]{1,0:T(8,128)} %get-tuple-element.92) | copy-start | bytes 1572868
  350.9 27.9 %copy-start.3 = (bf16[256,1024]{1,0:T(8,128)(2,1)S(1)}, bf16[256,1024]{1,0:T(8,128)(2,1)}, u32[]{:S(2)}) copy-start(bf16[256,1024]{1,0:T(8,128)(2,1)} %get-tuple-element.90) | copy-start | bytes 1572868
  350.9 27.9 %copy-start.4 = (bf16[256,1024]{1,0:T(8,128)(2,1)S(1)}, bf16[256,1024]{1,0:T(8,128)(2,1)}, u32[]{:S(2)}) copy-start(bf16[256,1024]{1,0:T(8,128)(2,1)} %get-tuple-element.91) | copy-start | bytes 1572868
  374.0 24.3 %all-to-all-start.5 = ((bf16[16,384,128]{2,1,0:T(8,128)(2,1)}), bf16[16,384,128]{2,1,0:T(8,128)(2,1)}, u32[]{:S(2)}, u32[]{:S(2)}) async-start(bf16[16,384,128]{2,1,0:T(8,128)(2,1)} %get-tuple-element.83), calls=%async_computation.5 | async-start | bytes 3145728 | tf_op jit(solution)/shard_map/all_to_all | solution.py:418
  378.4 151.5 %all-reduce.10.cloned.1.call-start = ((), (), s32[]{:S(2)}) async-start(), calls=%async_computation.12 | async-start | bytes 18874368
  415.7 189.8 %reduce-scatter.10.cloned.1.call-start = ((), (), s32[]{:S(2)}) async-start(), calls=%async_computation.13 | async-start | bytes 1253376
  532.9 169.4 %reduce-scatter.8.cloned.1.call-start = ((), (), s32[]{:S(2)}) async-start(), calls=%async_computation.8 | async-start | bytes 19464192 | tf_op jit(solution)/shard_map/reduce_scatter | solution.py:516
Sparse Core Ops, SparseCore 0:
  14.9 45.5 all-gather.6
  62.2 54.5 all-gather.8
  118.5 87.5 all-gather.10
  415.9 113.9 all-reduce.9
  533.5 71.9 reduce-scatter.9
  607.8 94.3 reduce-scatter.7
